TPU v7x, 128 devices: a whole 4x4x4 slice. The times are simulated.
128 devices in a mesh: row: 8 (over y_lo, z), col: 16 (over x, y_hi, core).
Axes of the slice: x: 4, y: 4 (y_hi: 2, y_lo: 2; y = y_hi * 2 + y_lo), z: 4, core: 2. Of those that a mesh axis runs over, the one named last changes fastest.
Arguments:
- image_embeds: float32 [16384, 1280], P(('row', 'col')), may hold values from -100 to 100
- text_embeds: float32 [16384, 1280], P(('col', 'row')), may hold values from -100 to 100
Outputs:
- image_grad: float32 [16384, 1280], P(('row', 'col'))
- text_grad: float32 [16384, 1280], P(('col', 'row'))
- loss: float32 [], replicated
All inputs are finite; a program needn't handle non-finite values.
Results may differ from a plain program's by a relative error of at most 0.0076.
Values may be sent and summed in bfloat16 or wider, within the bound.
No kernel may reach another device: no remote copies, remote signals or barrier semaphores. Data moves between devices by JAX's collectives and lax.ppermute only.
A program may use at most 128 MiB of HBM per device.

v0:
```python
import math

import jax
import jax.numpy as jnp
from jax import lax
from jax.sharding import PartitionSpec as P

LOGIT_SCALE = 100.0


def unit_rows(values):
    norms = jnp.sqrt(jnp.sum(values * values, axis=1, keepdims=True) + 1e-06)
    return (values / norms, norms)


def pair_scores(rows_bf, cols_bf):
    return LOGIT_SCALE * jnp.einsum(
        "ie,je->ij", rows_bf, cols_bf, preferred_element_type=jnp.float32
    )


def pair_weights(scores, lse_rows, lse_cols, row_ids, col_ids):
    matched = (row_ids[:, None] == col_ids[None, :]).astype(jnp.float32)
    summed = (
        jnp.exp(scores - lse_rows[:, None]) + jnp.exp(scores - lse_cols[None, :]) - 2.0 * matched
    )
    return (summed * 0.5).astype(jnp.bfloat16)


def per_device(image_embeds, text_embeds):
    own_rows = image_embeds.shape[0]
    image_unit, image_norm = unit_rows(image_embeds)
    text_unit, text_norm = unit_rows(text_embeds)
    image_block = unit_rows(lax.all_gather(image_embeds, "col", axis=0, tiled=True))[0].astype(
        jnp.bfloat16
    )
    text_block = unit_rows(lax.all_gather(text_embeds, "row", axis=0, tiled=True))[0].astype(
        jnp.bfloat16
    )
    tile_rows = image_block.shape[0]
    tile_cols = text_block.shape[0]
    width = image_block.shape[1]
    batch = tile_rows * lax.axis_size("row")
    row_base = lax.axis_index("row") * tile_rows
    col_base = lax.axis_index("col") * tile_cols
    block_rows = math.gcd(tile_rows, 512)
    blocks = tile_rows // block_rows
    col_ids = col_base + jnp.arange(tile_cols, dtype=jnp.int32)

    def forward(carried, step_index):
        anchor = step_index * block_rows
        rows_bf = lax.dynamic_slice_in_dim(image_block, anchor, block_rows, 0)
        scores = pair_scores(rows_bf, text_block)
        row_peak = jnp.max(scores, axis=1)
        row_total = jnp.sum(jnp.exp(scores - row_peak[:, None]), axis=1)
        col_peak, col_total, diag_sum = carried
        new_peak = jnp.maximum(col_peak, jnp.max(scores, axis=0))
        col_total = col_total * jnp.exp(col_peak - new_peak) + jnp.sum(
            jnp.exp(scores - new_peak[None, :]), axis=0
        )
        row_ids = row_base + anchor + jnp.arange(block_rows, dtype=jnp.int32)
        matched = row_ids[:, None] == col_ids[None, :]
        diag_sum = diag_sum + jnp.sum(jnp.where(matched, scores, jnp.zeros_like(scores)))
        return ((new_peak, col_total, diag_sum), (row_peak, row_total))

    initial = (
        jnp.full((tile_cols,), -jnp.inf, jnp.float32),
        jnp.zeros((tile_cols,), jnp.float32),
        jnp.zeros((), jnp.float32),
    )
    (col_peak, col_total, diag_sum), (row_peak, row_total) = lax.scan(
        forward, initial, jnp.arange(blocks, dtype=jnp.int32)
    )
    row_peak = row_peak.reshape(tile_rows)
    row_total = row_total.reshape(tile_rows)
    row_high = lax.pmax(row_peak, "col")
    row_sum = lax.psum(row_total * jnp.exp(row_peak - row_high), "col")
    col_high = lax.pmax(col_peak, "row")
    col_sum = lax.psum(col_total * jnp.exp(col_peak - col_high), "row")
    row_lse = row_high + jnp.log(row_sum)
    col_lse = col_high + jnp.log(col_sum)
    own_part = jnp.sum(
        lax.dynamic_slice_in_dim(row_lse, lax.axis_index("col") * own_rows, own_rows, 0)
    )
    own_part = own_part + jnp.sum(
        lax.dynamic_slice_in_dim(col_lse, lax.axis_index("row") * own_rows, own_rows, 0)
    )
    own_part = own_part - 2.0 * diag_sum
    loss = lax.psum(own_part, ("row", "col")) / (2.0 * batch)

    def backward(text_running, step_index):
        anchor = step_index * block_rows
        rows_bf = lax.dynamic_slice_in_dim(image_block, anchor, block_rows, 0)
        scores = pair_scores(rows_bf, text_block)
        row_ids = row_base + anchor + jnp.arange(block_rows, dtype=jnp.int32)
        weights = pair_weights(
            scores,
            lax.dynamic_slice_in_dim(row_lse, anchor, block_rows, 0),
            col_lse,
            row_ids,
            col_ids,
        )
        image_part = jnp.dot(weights, text_block, preferred_element_type=jnp.float32)
        text_running = text_running + jnp.einsum(
            "ij,ie->je", weights, rows_bf, preferred_element_type=jnp.float32
        )
        return (text_running, image_part)

    text_partial, image_parts = lax.scan(
        backward, jnp.zeros((tile_cols, width), jnp.float32), jnp.arange(blocks, dtype=jnp.int32)
    )
    image_partial = image_parts.reshape(tile_rows, width)
    image_dir = lax.psum_scatter(image_partial, "col", scatter_dimension=0, tiled=True)
    text_dir = lax.psum_scatter(text_partial, "row", scatter_dimension=0, tiled=True)
    image_grad = (
        image_dir - image_unit * jnp.sum(image_unit * image_dir, axis=1, keepdims=True)
    ) / image_norm
    text_grad = (
        text_dir - text_unit * jnp.sum(text_unit * text_dir, axis=1, keepdims=True)
    ) / text_norm
    return (image_grad, text_grad, loss)


def solution(mesh):
    return jax.shard_map(
        per_device,
        mesh=mesh,
        in_specs=(P(("row", "col"), None), P(("col", "row"), None)),
        out_specs=(P(("row", "col"), None), P(("col", "row"), None), P()),
        check_vma=False,
    )
```

profile of v0, /device:TPU:6, one launch (start us, length us, event | category | flops | bytes accessed | tf_op | source)
XLA Modules:
  0.0 546.8 jit_solution(4607580584507827063)
XLA Ops:
  8.8 65.9 %all-gather.5.cloned.1.call-done = f32[1024,1280]{1,0:T(8,128)} async-done(((f32[128,1280]{1,0:T(8,128)}), f32[1024,1280]{1,0:T(8,128)}) %all-gather.5.cloned.1.call-update) | async-done | bytes 5242896 | tf_op jit(solution)/shard_map/all_gather | solution.py:37
  80.8 74.5 %all-gather.3.cloned.1.call-done = f32[2048,1280]{1,0:T(8,128)} async-done(((f32[128,1280]{1,0:T(8,128)}), f32[2048,1280]{1,0:T(8,128)}) %all-gather.3.cloned.1.call-update) | async-done | bytes 10485776 | tf_op jit(solution)/shard_map/all_gather | solution.py:34
  155.3 4.9 multiply_reduce_fusion
  162.2 3.5 divide_convert_fusion
  165.7 30.3 %while.32 = (s32[]{:T(128)}, f32[1024]{0:T(1024)S(1)}, f32[1024]{0:T(1024)S(1)}, f32[]{:T(128)}, f32[4,512]{1,0:T(4,128)S(1)}, /*index=5*/f32[4,512]{1,0:T(4,128...) while((s32[]{:T(128)}, f32[1024]{0:T(1024)S(1)}, ...), condition=%wide.region_8.0_spmd.clone, body=%wide.region_2.8_spmd.clone.sunk | while | flops 1347425792 | bytes 8206594 | solution.py:71
  167.0 3.8 fusion.29
  174.6 3.8 fusion.29
  182.2 3.8 fusion.29
  189.7 3.8 fusion.29
  196.0 18.9 %pmax.15 = f32[1024]{0:T(1024)S(1)} all-reduce(f32[1024]{0:T(1024)S(1)} %get-tuple-element.119), channel_id=1, replica_groups=mesh['row'=8,'col'=16] {'row'}, use_global_device_ids=true, to_apply=%region_11.12 | all-reduce | flops 1024 | bytes 8192 | tf_op jit(solution)/shard_map/pmax | solution.py:78
  214.9 16.0 %psum.22 = f32[1024]{0:T(1024)S(1)} all-reduce(f32[1024]{0:T(1024)S(1)} %exponential_multiply_fusion.1), channel_id=1, replica_groups=mesh['row'=8,'col'=16] {'row'}, use_global_device_ids=true, to_apply=%region_12.13 | all-reduce | flops 1024 | bytes 8192 | tf_op jit(solution)/shard_map/psum | solution.py:79
  230.9 28.8 %pmax.14 = f32[2048]{0:T(1024)S(1)} all-reduce(f32[2048]{0:T(1024)S(1)} %bitcast.40), channel_id=1, replica_groups=mesh['row'=8,'col'=16] {'col'}, use_global_device_ids=true, to_apply=%region_9.10 | all-reduce | flops 2048 | bytes 16384 | tf_op jit(solution)/shard_map/pmax | solution.py:76
  259.8 31.5 %psum.21 = f32[2048]{0:T(1024)S(1)} all-reduce(f32[2048]{0:T(1024)S(1)} %exponential_multiply_fusion), channel_id=1, replica_groups=mesh['row'=8,'col'=16] {'col'}, use_global_device_ids=true, to_apply=%region_10.11 | all-reduce | flops 2048 | bytes 16384 | tf_op jit(solution)/shard_map/psum | solution.py:77
  291.3 60.7 %while.33 = (s32[]{:T(128)}, f32[1024,1280]{1,0:T(8,128)}, f32[4,512,1280]{2,1,0:T(8,128)}, s32[4]{0:T(128)S(1)}, bf16[2048,1280]{1,0:T(8,128)(2,1)}, /*index=5*...) while((s32[]{:T(128)}, f32[1024,1280]{1,0:T(8,128)}, ...), condition=%wide.region_14.15_spmd.clone, body=%wide.region_13.14_spmd.clone.sunk | while | flops 4033873408 | bytes 34626308 | solution.py:109
  292.6 4.3 multiply_convert_fusion.2
  300.1 5.2 select_add_fusion.2
  306.6 4.4 multiply_convert_fusion.2
  314.1 6.8 %select_add_fusion.2 = f32[1024,1280]{1,0:T(8,128)} fusion(f32[1024,1280]{1,0:T(8,128)} %get-tuple-element.447, bf16[512,1024]{1,0:T(8,128)(2,1)S(1)} %multiply_convert_fusion.2, pred[]{:T(512)S(6)} %compare.7, bf16[2048,1280]{1,0:T(8,128)(2,1)} %get-tuple-element.464, s32[]{:T(128)S(6)} %select_n.26), kind=kOutput, calls=%fused_computation.13.clone.1 | convolution fusion | flops 1344798720 | bytes 12845061 | tf_op jit(solution)/shard_map/while/body/eval_jaxpr/ij,ie->je/dot_general | solution.py:104
  322.2 4.4 multiply_convert_fusion.2
  329.6 6.8 %select_add_fusion.2 = f32[1024,1280]{1,0:T(8,128)} fusion(f32[1024,1280]{1,0:T(8,128)} %get-tuple-element.447, bf16[512,1024]{1,0:T(8,128)(2,1)S(1)} %multiply_convert_fusion.2, pred[]{:T(512)S(6)} %compare.7, bf16[2048,1280]{1,0:T(8,128)(2,1)} %get-tuple-element.464, s32[]{:T(128)S(6)} %select_n.26), kind=kOutput, calls=%fused_computation.13.clone.1 | convolution fusion | flops 1344798720 | bytes 12845061 | tf_op jit(solution)/shard_map/while/body/eval_jaxpr/ij,ie->je/dot_general | solution.py:104
  337.7 4.3 multiply_convert_fusion.2
  345.2 6.8 %select_add_fusion.2 = f32[1024,1280]{1,0:T(8,128)} fusion(f32[1024,1280]{1,0:T(8,128)} %get-tuple-element.447, bf16[512,1024]{1,0:T(8,128)(2,1)S(1)} %multiply_convert_fusion.2, pred[]{:T(512)S(6)} %compare.7, bf16[2048,1280]{1,0:T(8,128)(2,1)} %get-tuple-element.464, s32[]{:T(128)S(6)} %select_n.26), kind=kOutput, calls=%fused_computation.13.clone.1 | convolution fusion | flops 1344798720 | bytes 12845061 | tf_op jit(solution)/shard_map/while/body/eval_jaxpr/ij,ie->je/dot_general | solution.py:104
  356.1 110.7 %psum.23 = f32[]{:T(128)} all-reduce(f32[]{:T(128)S(6)} %sub.57), channel_id=1, replica_groups=mesh['row'=8,'col'=16] {'row','col'}, use_global_device_ids=true, to_apply=%region_23.24 | all-reduce | flops 1 | bytes 8 | tf_op jit(solution)/shard_map/psum | solution.py:89
  470.9 64.8 %reduce-scatter.3.cloned.1.call-done = f32[128,1280]{1,0:T(8,128)} async-done(((f32[2048,1280]{1,0:T(8,128)}), f32[128,1280]{1,0:T(8,128)}) %reduce-scatter.3.cloned.1.call-update) | async-done | bytes 655376 | tf_op jit(solution)/shard_map/reduce_scatter | solution.py:113
  (109 shorter events, 44.1 us)
Async XLA Ops:
  7.2 67.5 %all-gather.5.cloned.1.call-start = ((), (), s32[]{:S(2)}) async-start(), calls=%async_computation.3 | async-start | bytes 5898240 | tf_op jit(solution)/shard_map/all_gather | solution.py:37
  7.9 147.4 %all-gather.3.cloned.1.call-start = ((), (), s32[]{:S(2)}) async-start(), calls=%async_computation.2 | async-start | bytes 11141120 | tf_op jit(solution)/shard_map/all_gather | solution.py:34
  8.6 458.8 %reduce-scatter.5.cloned.1.call-start = ((), (), s32[]{:S(2)}) async-start(), calls=%async_computation.5 | async-start | bytes 5898240 | tf_op jit(solution)/shard_map/reduce_scatter | solution.py:114
  74.6 4.0 copy-start.1
  155.3 7.0 %copy-start = (f32[2048,1280]{1,0:T(8,128)S(1)}, f32[2048,1280]{1,0:T(8,128)}, u32[]{:S(2)}) copy-start(f32[2048,1280]{1,0:T(8,128)} %all-gather.3.cloned.1.call-done) | copy-start | bytes 31457284
  292.6 4.4 copy-start.4
  306.6 4.4 copy-start.4
  322.2 4.4 copy-start.4
  337.7 4.4 copy-start.4
  352.0 183.7 %reduce-scatter.3.cloned.1.call-start = ((), (), s32[]{:S(2)}) async-start(), calls=%async_computation.4 | async-start | bytes 11141120 | tf_op jit(solution)/shard_map/reduce_scatter | solution.py:113
  352.1 1.1 copy-start.2
  352.1 1.3 copy-start.3
Sparse Core Ops, SparseCore 0:
  9.6 64.9 all-gather.4
  77.0 78.2 all-gather.2
  352.1 68.7 reduce-scatter.4
  425.2 110.4 reduce-scatter.2
where the time goes:
time: 548 us; the launch traced here: 547 us
  waiting for transfers between devices  207 us (38%)
  blocking collectives  206 us (38%)
  matrix products  70.4 us (13%)
  other arithmetic  28.8 us (5%)
  between operations  17 us (3%)
  local copies, waits for them, and re-layouts  9.3 us (2%)
  loops' own time  8.09 us (1%)
    psum x1, blocking collectives, per_device(): loss = lax.psum(own_part, ('row', 'col')) / (2.0 * batch)  111 us
    all_gather x1, waiting for transfers between devices, per_device(): lax.all_gather(image_embeds, 'col', axis=0, tiled=True)  74.5 us
    all_gather x1, waiting for transfers between devices, per_device(): lax.all_gather(text_embeds, 'row', axis=0, tiled=True)  65.9 us
    reduce_scatter x1, waiting for transfers between devices, per_device(): lax.psum_scatter(image_partial, 'col', scatter_dimension=0, tiled=True)  64.8 us
    dot_general x8, matrix products, pair_scores(): jnp.einsum('ie,je->ij', rows_bf, cols_bf, preferred_element_type=jnp.floa...  32.5 us
    psum x1, blocking collectives, per_device(): row_sum = lax.psum(row_total * jnp.exp(row_peak - row_high), 'col')  31.5 us
    pmax x1, blocking collectives, per_device(): row_high = lax.pmax(row_peak, 'col')  28.8 us
    dot_general x4, matrix products, backward(): jnp.einsum('ij,ie->je', weights, rows_bf, preferred_element_type=jnp.floa...  25.6 us
  transfers between devices with their start and end apart: 4, of which 3 were waited for; matrix products, arithmetic and copies ran while one was open for 2% of the time, Pallas kernels for 0%

commit v1 on v0

v1 whole, which is shorter than its diff:
```python
import functools
import math

import jax
import jax.numpy as jnp
from jax import lax
from jax.experimental import pallas as pl
from jax.experimental.pallas import tpu as pltpu
from jax.sharding import PartitionSpec as P

PIECE = 128
WIDTH = 1280
XS, YS, KS, ZS = 4, 2, 2, 4
IMG = XS * YS * KS
TXT = ZS * YS

SHIFT = 22.0
LIFT = 70.0
FLOOR = math.exp(-62.0)
LOG2E = math.log2(math.e)

ANY = pl.BlockSpec(memory_space=pl.ANY)
VM = pl.BlockSpec(memory_space=pltpu.VMEM)
SM = pl.BlockSpec(memory_space=pltpu.SMEM)
PARAMS = pltpu.CompilerParams(vmem_limit_bytes=48 * 1024 * 1024)
F32, BF = jnp.float32, jnp.bfloat16
NT = (((1,), (1,)), ((), ()))
NN = (((1,), (0,)), ((), ()))
TN = (((0,), (0,)), ((), ()))


def dot(a, b, dims):
    return lax.dot_general(a, b, dims, preferred_element_type=F32)


def col_index(x, y, k):
    return (x * YS + y) * KS + k


def col_perm(dx, dy, dk):
    return [
        (col_index(x, y, k), col_index((x + dx) % XS, y ^ dy, k ^ dk))
        for x in range(XS)
        for y in range(YS)
        for k in range(KS)
    ]


def row_perm(dz, dy):
    return [(y * ZS + z, (y ^ dy) * ZS + (z + dz) % ZS) for y in range(YS) for z in range(ZS)]


def send_col(value, dx=0, dy=0, dk=0):
    return lax.ppermute(value, "col", col_perm(dx, dy, dk))


def send_row(value, dz=0, dy=0):
    return lax.ppermute(value, "row", row_perm(dz, dy))


def sum_col(value):
    value = value + send_col(value, dk=1)
    value = value + send_col(value, dx=1) + send_col(value, dx=2) + send_col(value, dx=3)
    return value + send_col(value, dy=1)


def sum_row(value):
    value = value + send_row(value, dz=1) + send_row(value, dz=2) + send_row(value, dz=3)
    return value + send_row(value, dy=1)


def cost(flops, bytes_accessed):
    return pl.CostEstimate(flops=flops, bytes_accessed=bytes_accessed, transcendentals=0)


def unit_kernel(image_ref, text_ref, image_out, text_out):
    for src, dst in ((image_ref, image_out), (text_ref, text_out)):
        x = src[...]
        dst[...] = (x / jnp.sqrt(jnp.sum(x * x, axis=1, keepdims=True) + 1e-06)).astype(BF)


def unit_pair(image, text):
    shape = jax.ShapeDtypeStruct((PIECE, WIDTH), BF)
    return pl.pallas_call(
        unit_kernel, out_shape=(shape, shape), in_specs=[VM, VM], out_specs=(VM, VM),
        compiler_params=PARAMS, name="unit_rows",
    )(image, text)


def forward_kernel(ids, *refs):
    img_in, txt_in = refs[:IMG], refs[IMG:IMG + TXT]
    h_own, h_oth, rs_out, cs_out, dg_out = refs[IMG + TXT:IMG + TXT + 5]
    img, txt, half, cacc, img_sem, txt_sem, out_sem = refs[IMG + TXT + 5:]
    txt_cp = [
        pltpu.make_async_copy(txt_in[q], txt.at[pl.ds(q * PIECE, PIECE)], txt_sem.at[q])
        for q in range(TXT)
    ]
    img_cp = [pltpu.make_async_copy(img_in[p], img.at[p], img_sem.at[p]) for p in range(IMG)]
    img_cp[0].start()
    img_cp[1].start()
    for c in txt_cp:
        c.start()
    for c in img_cp[2:]:
        c.start()
    cacc[...] = jnp.zeros_like(cacc)
    dg_out[...] = jnp.zeros_like(dg_out)
    for c in txt_cp:
        c.wait()
    eye = (
        lax.broadcasted_iota(jnp.int32, (PIECE, PIECE), 0)
        == lax.broadcasted_iota(jnp.int32, (PIECE, PIECE), 1)
    )

    @pl.loop(0, IMG // 2)
    def _(i):
        rows = []
        for u in range(2):
            p = 2 * i + u
            pltpu.make_async_copy(img.at[p], img.at[p], img_sem.at[p]).wait()
        block = img[pl.ds(2 * i, 2)].reshape(2 * PIECE, WIDTH)
        racc = [jnp.zeros((2 * PIECE, PIECE), F32) for _ in range(2)]
        for n in range(4):
            cols = pl.ds(n * 256, 256)
            d = dot(block, txt[cols, :], NT)
            h = jnp.exp2(d * (50.0 * LOG2E) - (0.5 * SHIFT * LOG2E))
            half[pl.ds(2 * i, 2), :, cols] = h.reshape(2, PIECE, 256)
            g = h * math.exp(0.5 * (SHIFT + LIFT))
            for t, v in enumerate((h * h, g * g)):
                racc[t] += v[:, :PIECE] + v[:, PIECE:]
                cacc[t, :, cols] += jnp.sum(v.reshape(32, 8, 256), axis=0)
        for u in range(2):
            p = 2 * i + u
            at = pl.ds(ids[p], 1)
            for t in range(2):
                part = racc[t][u * PIECE:(u + 1) * PIECE]
                rs_out[t, at, :] = jnp.sum(part.T, axis=0, keepdims=True)

            @pl.when(ids[IMG + TXT + p] >= 0)
            def _():
                q = ids[IMG + TXT + p]
                other = txt[pl.ds(pl.multiple_of(q * PIECE, PIECE), PIECE), :]
                s = 100.0 * dot(img[p], other, NT)
                dg_out[...] += jnp.sum(jnp.where(eye, s, 0.0).reshape(16, 8, PIECE), axis=0)

        @pl.when(i < IMG // 4)
        def _():
            pltpu.make_async_copy(half.at[pl.ds(2 * i, 2)], h_own.at[pl.ds(2 * i, 2)], out_sem).start()

        @pl.when(i >= IMG // 4)
        def _():
            j = 2 * i - IMG // 2
            pltpu.make_async_copy(half.at[pl.ds(2 * i, 2)], h_oth.at[pl.ds(j, 2)], out_sem).start()

    for t in range(2):
        total = jnp.sum(cacc[t], axis=0, keepdims=True)
        for q in range(TXT):
            cs_out[t, pl.ds(ids[IMG + q], 1), :] = total[:, q * PIECE:(q + 1) * PIECE]
    pltpu.make_async_copy(half, half, out_sem).wait()


def forward(ids, img, txt):
    half = jax.ShapeDtypeStruct((IMG // 2, PIECE, TXT * PIECE), F32)
    return pl.pallas_call(
        forward_kernel,
        out_shape=(
            half, half,
            jax.ShapeDtypeStruct((2, IMG, PIECE), F32),
            jax.ShapeDtypeStruct((2, TXT, PIECE), F32),
            jax.ShapeDtypeStruct((8, PIECE), F32),
        ),
        in_specs=[SM] + [ANY] * (IMG + TXT),
        out_specs=(ANY, ANY, VM, VM, VM),
        scratch_shapes=[
            pltpu.VMEM((IMG, PIECE, WIDTH), BF),
            pltpu.VMEM((TXT * PIECE, WIDTH), BF),
            pltpu.VMEM((IMG, PIECE, TXT * PIECE), F32),
            pltpu.VMEM((2, 8, TXT * PIECE), F32),
            pltpu.SemaphoreType.DMA((IMG,)),
            pltpu.SemaphoreType.DMA((TXT,)),
            pltpu.SemaphoreType.DMA,
        ],
        compiler_params=PARAMS,
        cost_estimate=cost(2 * 2048 * 1024 * 1280, 16 << 20),
        name="pair_scores",
    )(ids, *img, *txt)


def lse_of(sums):
    return jnp.where(sums[0] >= FLOOR, SHIFT + jnp.log(sums[0]), jnp.log(sums[1]) - LIFT)


def half_kernel(base, ids, rs, cs, h_in, *refs):
    txt_in = refs[:TXT]
    w_out, p_out = refs[TXT:TXT + 2]
    txt, half, a_s, b_s, h_sem, txt_sem = refs[TXT + 2:]
    n_p = IMG // 2
    h_cp = [pltpu.make_async_copy(h_in.at[p], half.at[p], h_sem.at[p]) for p in range(n_p)]
    txt_cp = [
        pltpu.make_async_copy(txt_in[q], txt.at[pl.ds(q * PIECE, PIECE)], txt_sem.at[q])
        for q in range(TXT)
    ]
    for c in h_cp[:2] + txt_cp + h_cp[2:]:
        c.start()
    scale = math.sqrt(0.5)
    a_s[...] = scale * jnp.exp(0.5 * (SHIFT - lse_of(rs[...])))
    b_s[...] = scale * jnp.exp(0.5 * (SHIFT - lse_of(cs[...])))
    b = [b_s[pl.ds(ids[IMG + q], 1), :] for q in range(TXT)]
    for c in txt_cp:
        c.wait()

    def weights(p):
        a = jnp.broadcast_to(a_s[pl.ds(ids[base + p], 1), :], (PIECE, PIECE)).T
        for q in range(TXT):
            h = half[p, :, q * PIECE:(q + 1) * PIECE]
            u, v = h * a, h * b[q]
            w_out[pl.ds(p * PIECE, PIECE), q * PIECE:(q + 1) * PIECE] = (u * u + v * v).astype(BF)
        match = ids[IMG + TXT + base + p]

        @pl.when(match >= 0)
        def _():
            cols = pl.ds(pl.multiple_of(match * PIECE, PIECE), PIECE)
            h = half[p, :, cols]
            bm = b_s[pl.ds(ids[IMG + match], 1), :]
            u, v = h * a, h * bm
            eye = (
                lax.broadcasted_iota(jnp.int32, (PIECE, PIECE), 0)
                == lax.broadcasted_iota(jnp.int32, (PIECE, PIECE), 1)
            ).astype(F32)
            w_out[pl.ds(p * PIECE, PIECE), cols] = (u * u + v * v - eye).astype(BF)

    @pl.loop(0, n_p // 2)
    def _(i):
        for u in range(2):
            p = 2 * i + u
            pltpu.make_async_copy(half.at[p], half.at[p], h_sem.at[p]).wait()
            weights(p)
        rows = pl.ds(i * 256, 256)
        for n in range(5):
            cols = slice(n * 256, n * 256 + 256)
            p_out[rows, cols] = dot(w_out[rows, :], txt[:, cols], NN).astype(p_out.dtype)


def half_products(base, ids, rs, cs, h, txt, dtype):
    rows = IMG // 2 * PIECE
    return pl.pallas_call(
        functools.partial(half_kernel, base),
        out_shape=(
            jax.ShapeDtypeStruct((rows, TXT * PIECE), BF),
            jax.ShapeDtypeStruct((rows, WIDTH), dtype),
        ),
        in_specs=[SM, VM, VM] + [ANY] * (1 + TXT),
        out_specs=(VM, VM),
        scratch_shapes=[
            pltpu.VMEM((TXT * PIECE, WIDTH), BF),
            pltpu.VMEM((IMG // 2, PIECE, TXT * PIECE), F32),
            pltpu.VMEM((IMG, PIECE), F32),
            pltpu.VMEM((TXT, PIECE), F32),
            pltpu.SemaphoreType.DMA((IMG // 2,)),
            pltpu.SemaphoreType.DMA((TXT,)),
        ],
        compiler_params=PARAMS,
        cost_estimate=cost(2 * 1024 * 1024 * 1280, 8 << 20),
        name="image_products",
    )(ids, rs, cs, h, *txt)


def text_kernel(w_own, w_oth, *refs):
    img_in = refs[:IMG]
    outs = refs[IMG:IMG + TXT]
    img, wo, wt, img_sem, w_sem = refs[IMG + TXT:]
    half = IMG // 2 * PIECE
    w_cp = [
        pltpu.make_async_copy(w_own, wo, w_sem.at[0]),
        pltpu.make_async_copy(w_oth, wt, w_sem.at[1]),
    ]
    img_cp = [
        pltpu.make_async_copy(img_in[p], img.at[pl.ds(p * PIECE, PIECE)], img_sem.at[p])
        for p in range(IMG)
    ]
    w_cp[1].start()
    for c in img_cp[IMG // 2:]:
        c.start()
    w_cp[0].start()
    for c in img_cp[:IMG // 2]:
        c.start()
    for c in w_cp + img_cp:
        c.wait()
    for z in (2, 1, 3, 0):
        for n in range(5):
            cols = slice(n * 256, n * 256 + 256)
            lanes = slice(z * 256, z * 256 + 256)
            d = dot(wt[:, lanes], img[half:, cols], TN) + dot(wo[:, lanes], img[:half, cols], TN)
            for y in range(YS):
                out = outs[z * YS + y]
                out[:, cols] = d[y * PIECE:(y + 1) * PIECE].astype(out.dtype)


def text_products(w_own, w_oth, img):
    return pl.pallas_call(
        text_kernel,
        out_shape=tuple(
            jax.ShapeDtypeStruct((PIECE, WIDTH), F32 if q < YS else BF) for q in range(TXT)
        ),
        in_specs=[ANY] * (2 + IMG),
        out_specs=(VM,) * TXT,
        scratch_shapes=[
            pltpu.VMEM((IMG * PIECE, WIDTH), BF),
            pltpu.VMEM((IMG // 2 * PIECE, TXT * PIECE), BF),
            pltpu.VMEM((IMG // 2 * PIECE, TXT * PIECE), BF),
            pltpu.SemaphoreType.DMA((IMG,)),
            pltpu.SemaphoreType.DMA((2,)),
        ],
        compiler_params=PARAMS,
        cost_estimate=cost(2 * 2048 * 1024 * 1280, 12 << 20),
        name="text_products",
    )(w_own, w_oth, *img)


def grad_kernel(values_ref, *refs):
    out = refs[-1]
    total = refs[0][...].astype(F32)
    for r in refs[1:-1]:
        total = total + r[...].astype(F32)
    x = values_ref[...]
    norm = jnp.sqrt(jnp.sum(x * x, axis=1, keepdims=True) + 1e-06)
    unit = x / norm
    out[...] = (total - unit * jnp.sum(unit * total, axis=1, keepdims=True)) / norm


def grad_rows(values, parts):
    return pl.pallas_call(
        grad_kernel,
        out_shape=jax.ShapeDtypeStruct((PIECE, WIDTH), F32),
        in_specs=[VM] * (1 + len(parts)),
        out_specs=VM,
        compiler_params=PARAMS,
        name="grad_rows",
    )(values, *parts)


def gather_ring(own, flip, step):
    other = flip(own)
    left0, right0 = step(own, 1), step(own, 3)
    left1, right1 = step(other, 1), step(other, 3)
    far0, far1 = step(left0, 1), step(right1, 3)
    return [own, other, right0, right1, far0, far1, left0, left1]


def scatter_ring(parts, flip, step):
    (own, other, near0, near1, far0, far1, back0, back1) = parts
    through0, through1 = step(far0, 1), step(far1, 3)
    add = lambda a, b: (a.astype(F32) + b.astype(F32)).astype(BF)
    right1, left0 = step(near1, 1), step(back0, 3)
    right0 = step(add(near0, through0), 1)
    left1 = step(add(back1, through1), 3)
    back = flip((other + right1.astype(F32) + left1.astype(F32)).astype(BF))
    return [own, right0, left0, back]


def per_device(image_embeds, text_embeds):
    row, col = lax.axis_index("row"), lax.axis_index("col")
    x, y, k = col // 4, col // 2 % 2, col % 2
    yl, z = row // 4, row % 4
    img_ids = [
        col_index((x + dx) % XS, y ^ dy, k ^ dk)
        for dk in range(KS) for dx in range(XS) for dy in range(YS)
    ]
    txt_ids = [(yl ^ dy) * ZS + (z + dz) % ZS for dz in range(ZS) for dy in range(YS)]
    match = []
    for c in img_ids:
        t = c % TXT
        q = ((t % ZS - z) % ZS) * YS + ((t // ZS) ^ yl)
        match.append(jnp.where(2 * row + c // TXT == col, q, -1))
    ids = jnp.stack(img_ids + txt_ids + match).astype(jnp.int32)

    image_own, text_own = unit_pair(image_embeds, text_embeds)
    txt = gather_ring(
        text_own, lambda v: send_row(v, dy=1), lambda v, d: send_row(v, dz=d)
    )
    img = gather_ring(
        image_own, lambda v: send_col(v, dy=1), lambda v, d: send_col(v, dx=d)
    )
    img = img + [send_col(v, dk=1) for v in img]

    h_own, h_oth, rs, cs, dg = forward(ids, img, txt)
    rs, cs = sum_col(rs), sum_row(cs)

    w_oth, p_oth = half_products(IMG // 2, ids, rs, cs, h_oth, txt, BF)
    far = {d: send_col(p_oth[d * 256:(d + 1) * 256], dk=1) for d in (2, 1, 3, 0)}
    w_own, p_own = half_products(0, ids, rs, cs, h_own, txt, F32)
    t_parts = text_products(w_own, w_oth, img)

    parts = []
    for d in range(XS):
        both = p_own[d * 256:(d + 1) * 256] + far[d].astype(F32)
        for dy in range(YS):
            part = both[dy * PIECE:(dy + 1) * PIECE]
            parts.append(part if d == 0 else part.astype(BF))
    i_sum = scatter_ring(parts, lambda v: send_col(v, dy=1), lambda v, d: send_col(v, dx=d))
    t_sum = scatter_ring(
        list(t_parts), lambda v: send_row(v, dy=1), lambda v, d: send_row(v, dz=d)
    )
    image_grad = grad_rows(image_embeds, i_sum)
    text_grad = grad_rows(text_embeds, t_sum)

    own = jnp.sum(lse_of(rs)) / IMG + jnp.sum(lse_of(cs)) / TXT - 2.0 * jnp.sum(dg)
    total = sum_row(sum_col(jnp.full((8, PIECE), own, F32)))
    batch = TXT * IMG * PIECE
    loss = total[0, 0] / (2.0 * batch)
    return (image_grad, text_grad, loss)


def solution(mesh):
    return jax.shard_map(
        per_device,
        mesh=mesh,
        in_specs=(P(("row", "col"), None), P(("col", "row"), None)),
        out_specs=(P(("row", "col"), None), P(("col", "row"), None), P()),
        check_vma=False,
    )
```

time: 548 us -> 202 us (0.37)
  blocking collectives: 206 us -> 0 us
  waiting for transfers between devices: 207 us -> 67.1 us
  matrix products: 70.4 us -> 0 us
  starting transfers between devices: 0.16 us -> 69.9 us
  Pallas kernels: 0 us -> 42.8 us
  other arithmetic: 28.8 us -> 3.24 us
  between operations: 17 us -> 6.59 us
  loops' own time: 8.09 us -> 0 us
    psum x3 -> x0, blocking collectives: 158 us -> none  [the longest x1 111 us: per_device(): loss = lax.psum(own_part, ('row', 'col')) / (2.0 * batch)]
    all_gather x2 -> x0, waiting for transfers between devices: 140 us -> none  [the longest x1 74.5 us: per_device(): lax.all_gather(image_embeds, 'col', axis=0, tiled=True)]
    dot_general x16 -> x0, matrix products: 70.4 us -> none  [the longest x8 32.5 us: pair_scores(): jnp.einsum('ie,je->ij', rows_bf, cols_bf, preferred_element_type=jnp.floa...]
    ppermute x0 -> x58, starting transfers between devices: none -> 69.9 us  [the longest x22 36.8 us: send_row(): return lax.ppermute(value, 'row', row_perm(dz, dy))]
    ppermute x0 -> x58, waiting for transfers between devices: none -> 67.1 us  [the longest x22 33.8 us: send_row(): return lax.ppermute(value, 'row', row_perm(dz, dy))]
    reduce_scatter x2 -> x0, waiting for transfers between devices: 64.8 us -> none  [the longest x1 64.8 us: per_device(): lax.psum_scatter(image_partial, 'col', scatter_dimension=0, tiled=True)]
    pmax x2 -> x0, blocking collectives: 47.8 us -> none  [the longest x1 28.8 us: per_device(): row_high = lax.pmax(row_peak, 'col')]
    pallas_call x0 -> x7, Pallas kernels: none -> 42.8 us  [the longest x2 17.4 us: half_products(): pl.pallas_call(functools.partial(half_kernel, base), out_shape=(jax.Shape...]
  transfers between devices with their start and end apart: 4 -> 58, of which waited for: 3 -> 18; matrix products, arithmetic and copies ran while one was open for 2% -> 2% of each run, Pallas kernels for 0% -> 14%
where the time goes in v1:
time: 202 us
  starting transfers between devices  69.9 us (35%)
  waiting for transfers between devices  67.1 us (33%)
  Pallas kernels  42.8 us (21%)
  local copies, waits for them, and re-layouts  12.3 us (6%)
  between operations  6.59 us (3%)
  other arithmetic  3.24 us (2%)
    ppermute x22, starting transfers between devices, send_row(): return lax.ppermute(value, 'row', row_perm(dz, dy))  36.8 us
    ppermute x22, waiting for transfers between devices, send_row(): return lax.ppermute(value, 'row', row_perm(dz, dy))  33.8 us
    ppermute x36, waiting for transfers between devices, send_col(): return lax.ppermute(value, 'col', col_perm(dx, dy, dk))  33.4 us
    ppermute x36, starting transfers between devices, send_col(): return lax.ppermute(value, 'col', col_perm(dx, dy, dk))  33.1 us
    pallas_call x2, Pallas kernels, half_products(): pl.pallas_call(functools.partial(half_kernel, base), out_shape=(jax.Shape...  17.4 us
    pallas_call x1, Pallas kernels, forward(): pl.pallas_call(forward_kernel, out_shape=(half, half, jax.ShapeDtypeStruc...  12.6 us
    unnamed x46, local copies, waits for them, and re-layouts  11.4 us
    pallas_call x1, Pallas kernels, text_products(): pl.pallas_call(text_kernel, out_shape=tuple((jax.ShapeDtypeStruct((PIECE,...  10.1 us
  transfers between devices with their start and end apart: 58, of which 18 were waited for; matrix products, arithmetic and copies ran while one was open for 2% of the time, Pallas kernels for 14%

profile of v1, /device:TPU:6, one launch (start us, length us, event | category | flops | bytes accessed | tf_op | source)
XLA Modules:
  0.0 201.9 jit_solution(1892814449027097305)
XLA Ops:
  5.2 3.2 %collective-permute-start = (bf16[128,1280]{1,0:T(8,128)(2,1)S(1)}, bf16[128,1280]{1,0:T(8,128)(2,1)S(1)}, u32[]{:S(2)}, u32[]{:S(2)}) collective-permute-start(bf16[128,1280]{1,0:T(8,128)(2,1)S(1)} %get-tuple-element.22.refs_0_), channel_id=1, source_target_pairs={{0,2},{1,3},{2,0},{3,1},{4,6},{5,7},{6,4},{7,5},{8,10},{9,11},{10,... | collective-permute-start | bytes 983048 | tf_op jit(solution)/shard_map/ppermute | solution.py:54
  20.4 3.1 %collective-permute-done.15.refs_17_.refs_1_ = bf16[128,1280]{1,0:T(8,128)(2,1)S(1)} collective-permute-done((bf16[128,1280]{1,0:T(8,128)(2,1)S(1)}, bf16[128,1280]{1,0:T(8,128)(2,1)S(1)}, u32[]{:S(2)}, u32[]{:S(2)}) %collective-permute-start.15) | collective-permute-done | bytes 327712 | tf_op jit(solution)/shard_map/ppermute | solution.py:58
  33.6 5.8 %collective-permute-done.19.refs_20_.refs_4_ = bf16[128,1280]{1,0:T(8,128)(2,1)S(1)} collective-permute-done((bf16[128,1280]{1,0:T(8,128)(2,1)S(1)}, bf16[128,1280]{1,0:T(8,128)(2,1)S(1)}, u32[]{:S(2)}, u32[]{:S(2)}) %collective-permute-start.19) | collective-permute-done | bytes 327712 | tf_op jit(solution)/shard_map/ppermute | solution.py:58
  39.5 4.8 %collective-permute-done.21.refs_23_.refs_7_ = bf16[128,1280]{1,0:T(8,128)(2,1)S(1)} collective-permute-done((bf16[128,1280]{1,0:T(8,128)(2,1)S(1)}, bf16[128,1280]{1,0:T(8,128)(2,1)S(1)}, u32[]{:S(2)}, u32[]{:S(2)}) %collective-permute-start.21) | collective-permute-done | bytes 327712 | tf_op jit(solution)/shard_map/ppermute | solution.py:58
  48.2 6.5 %collective-permute-done.20.refs_21_.refs_5_ = bf16[128,1280]{1,0:T(8,128)(2,1)} collective-permute-done((bf16[128,1280]{1,0:T(8,128)(2,1)}, bf16[128,1280]{1,0:T(8,128)(2,1)}, u32[]{:S(2)}, u32[]{:S(2)}) %collective-permute-start.20) | collective-permute-done | bytes 327712 | tf_op jit(solution)/shard_map/ppermute | solution.py:58
  55.8 12.6 %pair_scores.1 = (f32[8,128,1024]{2,1,0:T(8,128)}, f32[8,128,1024]{2,1,0:T(8,128)}, f32[2,16,128]{2,1,0:T(8,128)S(1)}, f32[2,8,128]{2,1,0:T(8,128)S(1)}, f32[8,128]{1,0:T(8,128)S(1)}) custom-call(s32[40]{0:T(128)S(1)} %stack.163.ids, bf16[128,1280]{1,0:T(8,128)(2,1)S(1)} %get-tuple-element.22.refs_0_, bf16[128,1280]{1,0:T(8,128)(2,1)S(1)} %collective-permute-done.refs_1_, ...), custom_call_target="tpu_custom_call" | custom-call | flops 5368709120 | bytes 16777216 | tf_op jit(solution)/shard_map/pair_scores/pallas_call | solution.py:163
  68.5 3.0 %collective-permute-start.29 = (f32[2,8,128]{2,1,0:T(8,128)S(1)}, f32[2,8,128]{2,1,0:T(8,128)S(1)}, u32[]{:S(2)}, u32[]{:S(2)}) collective-permute-start(f32[2,8,128]{2,1,0:T(8,128)S(1)} %get-tuple-element.25), channel_id=1, source_target_pairs={{0,48},{16,0},{32,16},{48,32},{64,112},{80,64},{96,80},{112,96},{1... | collective-permute-start | bytes 24584 | tf_op jit(solution)/shard_map/ppermute | solution.py:58
  80.5 3.1 %collective-permute-start.26 = (f32[2,16,128]{2,1,0:T(8,128)S(1)}, f32[2,16,128]{2,1,0:T(8,128)S(1)}, u32[]{:S(2)}, u32[]{:S(2)}) collective-permute-start(f32[2,16,128]{2,1,0:T(8,128)S(1)} %add_add_fusion), channel_id=1, source_target_pairs={{0,2},{1,3},{2,0},{3,1},{4,6},{5,7},{6,4},{7,5},{8,10},{9,11},{10,... | collective-permute-start | bytes 49160 | tf_op jit(solution)/shard_map/ppermute | solution.py:54
  92.0 8.3 %image_products.3 = (bf16[1024,1024]{1,0:T(8,128)(2,1)S(1)}, bf16[1024,1280]{1,0:T(8,128)(2,1)}) custom-call(s32[40]{0:T(128)S(1)} %stack.163.ids, f32[2,16,128]{2,1,0:T(8,128)S(1)} %add.703.rs, f32[2,8,128]{2,1,0:T(8,128)S(1)} %add.707.cs, f32[8,128,1024]{2,1,0:T(8,128)} %get-tuple-element.28.h_in, ...), custom_call_target="tpu_custom_call" | custom-call | flops 2684354560 | bytes 8388608 | tf_op jit(solution)/shard_map/image_products/pallas_call | solution.py:245
  101.7 2.8 %collective-permute-start.51 = (f32[8,128]{1,0:T(8,128)S(1)}, f32[8,128]{1,0:T(8,128)S(1)}, u32[]{:S(2)}, u32[]{:S(2)}) collective-permute-start(f32[8,128]{1,0:T(8,128)S(1)} %broadcast_add_fusion), channel_id=1, source_target_pairs={{0,8},{1,9},{2,10},{3,11},{4,12},{5,13},{6,14},{7,15},{8,0},{9,1},... | collective-permute-start | bytes 12296 | tf_op jit(solution)/shard_map/ppermute | solution.py:54
  104.5 3.2 %collective-permute-start.50 = (f32[8,128]{1,0:T(8,128)S(1)}, f32[8,128]{1,0:T(8,128)S(1)}, u32[]{:S(2)}, u32[]{:S(2)}) collective-permute-start(f32[8,128]{1,0:T(8,128)S(1)} %broadcast_add_fusion), channel_id=1, source_target_pairs={{0,4},{1,5},{2,6},{3,7},{4,8},{5,9},{6,10},{7,11},{8,12},{9,13},{1... | collective-permute-start | bytes 12296 | tf_op jit(solution)/shard_map/ppermute | solution.py:54
  107.7 9.1 %image_products.2 = (bf16[1024,1024]{1,0:T(8,128)(2,1)S(1)}, f32[1024,1280]{1,0:T(8,128)}) custom-call(s32[40]{0:T(128)S(1)} %stack.163.ids, f32[2,16,128]{2,1,0:T(8,128)S(1)} %add.703.rs, f32[2,8,128]{2,1,0:T(8,128)S(1)} %add.707.cs, f32[8,128,1024]{2,1,0:T(8,128)} %get-tuple-element.26.h_in, bf16[128,1280]{1,0:T(8,128)(2,1)S(1)} %get-tuple-element.23.refs_16_.refs_0_, ...), custom_call_target="tpu_custom_call" | custom-call | flops 2684354560 | bytes 8388608 | tf_op jit(solution)/shard_map/image_products/pallas_call | solution.py:245
  120.7 10.1 %text_products.1 = (f32[128,1280]{1,0:T(8,128)}, f32[128,1280]{1,0:T(8,128)}, bf16[128,1280]{1,0:T(8,128)(2,1)S(1)}, bf16[128,1280]{1,0:T(8,128)(2,1)S(1)}, bf16...) custom-call(bf16[1024,1024]{1,0:T(8,128)(2,1)} %copy-done.18, ...), custom_call_target="tpu_custom_call" | custom-call | flops 5368709120 | bytes 12582912 | tf_op jit(solution)/shard_map/text_products/pallas_call | solution.py:299
  130.8 2.6 %collective-permute-start.42 = (bf16[128,1280]{1,0:T(8,128)(2,1)S(1)}, bf16[128,1280]{1,0:T(8,128)(2,1)S(1)}, u32[]{:S(2)}, u32[]{:S(2)}) collective-permute-start(bf16[128,1280]{1,0:T(8,128)(2,1)S(1)} %get-tuple-element.34), channel_id=1, source_target_pairs={{0,16},{16,32},{32,48},{48,0},{64,80},{80,96},{96,112},{112,64},{1... | collective-permute-start | bytes 983048 | tf_op jit(solution)/shard_map/ppermute | solution.py:58
  136.3 3.0 %collective-permute-start.46 = (bf16[128,1280]{1,0:T(8,128)(2,1)S(1)}, bf16[128,1280]{1,0:T(8,128)(2,1)S(1)}, u32[]{:S(2)}, u32[]{:S(2)}) collective-permute-start(bf16[128,1280]{1,0:T(8,128)(2,1)S(1)} %get-tuple-element.39), channel_id=1, source_target_pairs={{0,48},{16,0},{32,16},{48,32},{64,112},{80,64},{96,80},{112,96},{1... | collective-permute-start | bytes 983048 | tf_op jit(solution)/shard_map/ppermute | solution.py:58
  139.3 2.5 %collective-permute-done.55 = f32[8,128]{1,0:T(8,128)S(1)} collective-permute-done((f32[8,128]{1,0:T(8,128)S(1)}, f32[8,128]{1,0:T(8,128)S(1)}, u32[]{:S(2)}, u32[]{:S(2)}) %collective-permute-start.55) | collective-permute-done | bytes 4128 | tf_op jit(solution)/shard_map/ppermute | solution.py:58
  144.9 3.7 %collective-permute-start.44 = (bf16[128,1280]{1,0:T(8,128)(2,1)S(1)}, bf16[128,1280]{1,0:T(8,128)(2,1)S(1)}, u32[]{:S(2)}, u32[]{:S(2)}) collective-permute-start(bf16[128,1280]{1,0:T(8,128)(2,1)S(1)} %get-tuple-element.35), channel_id=1, source_target_pairs={{0,48},{16,0},{32,16},{48,32},{64,112},{80,64},{96,80},{112,96},{1... | collective-permute-start | bytes 983048 | tf_op jit(solution)/shard_map/ppermute | solution.py:58
  150.3 3.2 %collective-permute-start.47 = (bf16[128,1280]{1,0:T(8,128)(2,1)S(1)}, bf16[128,1280]{1,0:T(8,128)(2,1)S(1)}, u32[]{:S(2)}, u32[]{:S(2)}) collective-permute-start(bf16[128,1280]{1,0:T(8,128)(2,1)S(1)} %add_convert_fusion.4), channel_id=1, source_target_pairs={{0,48},{16,0},{32,16},{48,32},{64,112},{80,64},{96,80},{112,96},{1... | collective-permute-start | bytes 983048 | tf_op jit(solution)/shard_map/ppermute | solution.py:58
  154.5 5.9 %collective-permute-done.45 = bf16[128,1280]{1,0:T(8,128)(2,1)S(1)} collective-permute-done((bf16[128,1280]{1,0:T(8,128)(2,1)S(1)}, bf16[128,1280]{1,0:T(8,128)(2,1)S(1)}, u32[]{:S(2)}, u32[]{:S(2)}) %collective-permute-start.45) | collective-permute-done | bytes 327712 | tf_op jit(solution)/shard_map/ppermute | solution.py:58
  162.6 6.7 %collective-permute-done.39 = bf16[128,1280]{1,0:T(8,128)(2,1)S(1)} collective-permute-done((bf16[128,1280]{1,0:T(8,128)(2,1)S(1)}, bf16[128,1280]{1,0:T(8,128)(2,1)S(1)}, u32[]{:S(2)}, u32[]{:S(2)}) %collective-permute-start.39) | collective-permute-done | bytes 327712 | tf_op jit(solution)/shard_map/ppermute | solution.py:54
  169.4 7.0 %collective-permute-done.34 = bf16[128,1280]{1,0:T(8,128)(2,1)S(1)} collective-permute-done((bf16[128,1280]{1,0:T(8,128)(2,1)S(1)}, bf16[128,1280]{1,0:T(8,128)(2,1)S(1)}, u32[]{:S(2)}, u32[]{:S(2)}) %collective-permute-start.34) | collective-permute-done | bytes 327712 | tf_op jit(solution)/shard_map/ppermute | solution.py:54
  178.2 9.4 %collective-permute-done.40 = bf16[128,1280]{1,0:T(8,128)(2,1)S(1)} collective-permute-done((bf16[128,1280]{1,0:T(8,128)(2,1)S(1)}, bf16[128,1280]{1,0:T(8,128)(2,1)S(1)}, u32[]{:S(2)}, u32[]{:S(2)}) %collective-permute-start.40) | collective-permute-done | bytes 327712 | tf_op jit(solution)/shard_map/ppermute | solution.py:54
  187.7 3.3 %collective-permute-start.35 = (bf16[128,1280]{1,0:T(8,128)(2,1)S(1)}, bf16[128,1280]{1,0:T(8,128)(2,1)S(1)}, u32[]{:S(2)}, u32[]{:S(2)}) collective-permute-start(bf16[128,1280]{1,0:T(8,128)(2,1)S(1)} %add_convert_fusion.7), channel_id=1, source_target_pairs={{0,4},{1,5},{2,6},{3,7},{4,8},{5,9},{6,10},{7,11},{8,12},{9,13},{1... | collective-permute-start | bytes 983048 | tf_op jit(solution)/shard_map/ppermute | solution.py:54
  195.9 3.7 %collective-permute-done.41.refs_3_ = bf16[128,1280]{1,0:T(8,128)(2,1)S(1)} collective-permute-done((bf16[128,1280]{1,0:T(8,128)(2,1)S(1)}, bf16[128,1280]{1,0:T(8,128)(2,1)S(1)}, u32[]{:S(2)}, u32[]{:S(2)}) %collective-permute-start.41) | collective-permute-done | bytes 327712 | tf_op jit(solution)/shard_map/ppermute | solution.py:54
  (173 shorter events, 68.5 us)
Async XLA Ops:
  3.6 11.2 %collective-permute-start.1 = (bf16[128,1280]{1,0:T(8,128)(2,1)S(1)}, bf16[128,1280]{1,0:T(8,128)(2,1)S(1)}, u32[]{:S(2)}, u32[]{:S(2)}) collective-permute-start(bf16[128,1280]{1,0:T(8,128)(2,1)S(1)} %get-tuple-element.22.refs_0_), channel_id=1, source_target_pairs={{0,12},{1,13},{2,14},{3,15},{4,0},{5,1},{6,2},{7,3},{8,4},{9,5},{1... | collective-permute-start | bytes 983048 | tf_op jit(solution)/shard_map/ppermute | solution.py:54
  5.2 11.0 %collective-permute-start = (bf16[128,1280]{1,0:T(8,128)(2,1)S(1)}, bf16[128,1280]{1,0:T(8,128)(2,1)S(1)}, u32[]{:S(2)}, u32[]{:S(2)}) collective-permute-start(bf16[128,1280]{1,0:T(8,128)(2,1)S(1)} %get-tuple-element.22.refs_0_), channel_id=1, source_target_pairs={{0,2},{1,3},{2,0},{3,1},{4,6},{5,7},{6,4},{7,5},{8,10},{9,11},{10,... | collective-permute-start | bytes 983048 | tf_op jit(solution)/shard_map/ppermute | solution.py:54
  8.4 11.5 %collective-permute-start.18 = (bf16[128,1280]{1,0:T(8,128)(2,1)S(1)}, bf16[128,1280]{1,0:T(8,128)(2,1)S(1)}, u32[]{:S(2)}, u32[]{:S(2)}) collective-permute-start(bf16[128,1280]{1,0:T(8,128)(2,1)S(1)} %get-tuple-element.23.refs_16_.refs_0_), channel_id=1, source_target_pairs={{0,16},{16,32},{32,48},{48,0},{64,80},{80,96},{96,112},{112,64},{1... | collective-permute-start | bytes 983048 | tf_op jit(solution)/shard_map/ppermute | solution.py:58
  16.2 10.6 %collective-permute-start.4 = (bf16[128,1280]{1,0:T(8,128)(2,1)S(1)}, bf16[128,1280]{1,0:T(8,128)(2,1)S(1)}, u32[]{:S(2)}, u32[]{:S(2)}) collective-permute-start(bf16[128,1280]{1,0:T(8,128)(2,1)S(1)} %collective-permute-done.3.refs_6_), channel_id=1, source_target_pairs={{0,4},{1,5},{2,6},{3,7},{4,8},{5,9},{6,10},{7,11},{8,12},{9,13},{1... | collective-permute-start | bytes 983048 | tf_op jit(solution)/shard_map/ppermute | solution.py:54
  19.9 10.7 %collective-permute-start.8 = (bf16[128,1280]{1,0:T(8,128)(2,1)S(1)}, bf16[128,1280]{1,0:T(8,128)(2,1)S(1)}, u32[]{:S(2)}, u32[]{:S(2)}) collective-permute-start(bf16[128,1280]{1,0:T(8,128)(2,1)S(1)} %collective-permute-done.refs_1_), channel_id=1, source_target_pairs={{0,1},{1,0},{2,3},{3,2},{4,5},{5,4},{6,7},{7,6},{8,9},{9,8},{10,11... | collective-permute-start | bytes 983048 | tf_op jit(solution)/shard_map/ppermute | solution.py:54
  26.8 12.7 %collective-permute-start.19 = (bf16[128,1280]{1,0:T(8,128)(2,1)S(1)}, bf16[128,1280]{1,0:T(8,128)(2,1)S(1)}, u32[]{:S(2)}, u32[]{:S(2)}) collective-permute-start(bf16[128,1280]{1,0:T(8,128)(2,1)S(1)} %collective-permute-done.18.refs_22_.refs_6_), channel_id=1, source_target_pairs={{0,16},{16,32},{32,48},{48,0},{64,80},{80,96},{96,112},{112,64},{1... | collective-permute-start | bytes 983048 | tf_op jit(solution)/shard_map/ppermute | solution.py:58
  28.7 15.6 %collective-permute-start.21 = (bf16[128,1280]{1,0:T(8,128)(2,1)S(1)}, bf16[128,1280]{1,0:T(8,128)(2,1)S(1)}, u32[]{:S(2)}, u32[]{:S(2)}) collective-permute-start(bf16[128,1280]{1,0:T(8,128)(2,1)S(1)} %collective-permute-done.15.refs_17_.refs_1_), channel_id=1, source_target_pairs={{0,16},{16,32},{32,48},{48,0},{64,80},{80,96},{96,112},{112,64},{1... | collective-permute-start | bytes 983048 | tf_op jit(solution)/shard_map/ppermute | solution.py:58
  30.7 13.6 %collective-permute-start.17 = (bf16[128,1280]{1,0:T(8,128)(2,1)S(1)}, bf16[128,1280]{1,0:T(8,128)(2,1)}, u32[]{:S(2)}, u32[]{:S(2)}) collective-permute-start(bf16[128,1280]{1,0:T(8,128)(2,1)S(1)} %collective-permute-done.15.refs_17_.refs_1_), channel_id=1, source_target_pairs={{0,48},{16,0},{32,16},{48,32},{64,112},{80,64},{96,80},{112,96},{1... | collective-permute-start | bytes 983048 | tf_op jit(solution)/shard_map/ppermute | solution.py:58
  33.6 12.5 %collective-permute-start.5 = (bf16[128,1280]{1,0:T(8,128)(2,1)}, bf16[128,1280]{1,0:T(8,128)(2,1)}, u32[]{:S(2)}, u32[]{:S(2)}) collective-permute-start(bf16[128,1280]{1,0:T(8,128)(2,1)} %collective-permute-done.2.refs_3_), channel_id=1, source_target_pairs={{0,12},{1,13},{2,14},{3,15},{4,0},{5,1},{6,2},{7,3},{8,4},{9,5},{1... | collective-permute-start | bytes 983048 | tf_op jit(solution)/shard_map/ppermute | solution.py:54
  33.6 14.6 %collective-permute-start.10 = (bf16[128,1280]{1,0:T(8,128)(2,1)}, bf16[128,1280]{1,0:T(8,128)(2,1)}, u32[]{:S(2)}, u32[]{:S(2)}) collective-permute-start(bf16[128,1280]{1,0:T(8,128)(2,1)} %collective-permute-done.2.refs_3_), channel_id=1, source_target_pairs={{0,1},{1,0},{2,3},{3,2},{4,5},{5,4},{6,7},{7,6},{8,9},{9,8},{10,11... | collective-permute-start | bytes 983048 | tf_op jit(solution)/shard_map/ppermute | solution.py:54
  87.1 14.6 %collective-permute-start.49 = (f32[8,128]{1,0:T(8,128)S(1)}, f32[8,128]{1,0:T(8,128)S(1)}, u32[]{:S(2)}, u32[]{:S(2)}) collective-permute-start(f32[8,128]{1,0:T(8,128)S(1)} %broadcast_in_dim.3), channel_id=1, source_target_pairs={{0,1},{1,0},{2,3},{3,2},{4,5},{5,4},{6,7},{7,6},{8,9},{9,8},{10,11... | collective-permute-start | bytes 12296 | tf_op jit(solution)/shard_map/ppermute | solution.py:54
  101.7 16.5 %collective-permute-start.51 = (f32[8,128]{1,0:T(8,128)S(1)}, f32[8,128]{1,0:T(8,128)S(1)}, u32[]{:S(2)}, u32[]{:S(2)}) collective-permute-start(f32[8,128]{1,0:T(8,128)S(1)} %broadcast_add_fusion), channel_id=1, source_target_pairs={{0,8},{1,9},{2,10},{3,11},{4,12},{5,13},{6,14},{7,15},{8,0},{9,1},... | collective-permute-start | bytes 12296 | tf_op jit(solution)/shard_map/ppermute | solution.py:54
  104.5 13.7 %collective-permute-start.52 = (f32[8,128]{1,0:T(8,128)S(1)}, f32[8,128]{1,0:T(8,128)S(1)}, u32[]{:S(2)}, u32[]{:S(2)}) collective-permute-start(f32[8,128]{1,0:T(8,128)S(1)} %broadcast_add_fusion), channel_id=1, source_target_pairs={{0,12},{1,13},{2,14},{3,15},{4,0},{5,1},{6,2},{7,3},{8,4},{9,5},{1... | collective-permute-start | bytes 12296 | tf_op jit(solution)/shard_map/ppermute | solution.py:54
  104.5 13.7 %collective-permute-start.50 = (f32[8,128]{1,0:T(8,128)S(1)}, f32[8,128]{1,0:T(8,128)S(1)}, u32[]{:S(2)}, u32[]{:S(2)}) collective-permute-start(f32[8,128]{1,0:T(8,128)S(1)} %broadcast_add_fusion), channel_id=1, source_target_pairs={{0,4},{1,5},{2,6},{3,7},{4,8},{5,9},{6,10},{7,11},{8,12},{9,13},{1... | collective-permute-start | bytes 12296 | tf_op jit(solution)/shard_map/ppermute | solution.py:54
  118.2 15.2 %collective-permute-start.53 = (f32[8,128]{1,0:T(8,128)S(1)}, f32[8,128]{1,0:T(8,128)S(1)}, u32[]{:S(2)}, u32[]{:S(2)}) collective-permute-start(f32[8,128]{1,0:T(8,128)S(1)} %add_add_fusion.3), channel_id=1, source_target_pairs={{0,2},{1,3},{2,0},{3,1},{4,6},{5,7},{6,4},{7,5},{8,10},{9,11},{10,... | collective-permute-start | bytes 12296 | tf_op jit(solution)/shard_map/ppermute | solution.py:54
  130.8 11.5 %collective-permute-start.42 = (bf16[128,1280]{1,0:T(8,128)(2,1)S(1)}, bf16[128,1280]{1,0:T(8,128)(2,1)S(1)}, u32[]{:S(2)}, u32[]{:S(2)}) collective-permute-start(bf16[128,1280]{1,0:T(8,128)(2,1)S(1)} %get-tuple-element.34), channel_id=1, source_target_pairs={{0,16},{16,32},{32,48},{48,0},{64,80},{80,96},{96,112},{112,64},{1... | collective-permute-start | bytes 983048 | tf_op jit(solution)/shard_map/ppermute | solution.py:58
  144.9 46.1 %collective-permute-start.44 = (bf16[128,1280]{1,0:T(8,128)(2,1)S(1)}, bf16[128,1280]{1,0:T(8,128)(2,1)S(1)}, u32[]{:S(2)}, u32[]{:S(2)}) collective-permute-start(bf16[128,1280]{1,0:T(8,128)(2,1)S(1)} %get-tuple-element.35), channel_id=1, source_target_pairs={{0,48},{16,0},{32,16},{48,32},{64,112},{80,64},{96,80},{112,96},{1... | collective-permute-start | bytes 983048 | tf_op jit(solution)/shard_map/ppermute | solution.py:58
  148.7 11.7 %collective-permute-start.45 = (bf16[128,1280]{1,0:T(8,128)(2,1)S(1)}, bf16[128,1280]{1,0:T(8,128)(2,1)S(1)}, u32[]{:S(2)}, u32[]{:S(2)}) collective-permute-start(bf16[128,1280]{1,0:T(8,128)(2,1)S(1)} %get-tuple-element.37), channel_id=1, source_target_pairs={{0,16},{16,32},{32,48},{48,0},{64,80},{80,96},{96,112},{112,64},{1... | collective-permute-start | bytes 983048 | tf_op jit(solution)/shard_map/ppermute | solution.py:58
  148.8 38.9 %collective-permute-start.57 = (f32[8,128]{1,0:T(8,128)S(1)}, f32[8,128]{1,0:T(8,128)S(1)}, u32[]{:S(2)}, u32[]{:S(2)}) collective-permute-start(f32[8,128]{1,0:T(8,128)S(1)} %add_add_fusion.2), channel_id=1, source_target_pairs={{0,64},{16,80},{32,96},{48,112},{64,0},{80,16},{96,32},{112,48},{1... | collective-permute-start | bytes 12296 | tf_op jit(solution)/shard_map/ppermute | solution.py:58
  150.3 41.9 %collective-permute-start.43 = (bf16[128,1280]{1,0:T(8,128)(2,1)S(1)}, bf16[128,1280]{1,0:T(8,128)(2,1)S(1)}, u32[]{:S(2)}, u32[]{:S(2)}) collective-permute-start(bf16[128,1280]{1,0:T(8,128)(2,1)S(1)} %add_convert_fusion.5), channel_id=1, source_target_pairs={{0,16},{16,32},{32,48},{48,0},{64,80},{80,96},{96,112},{112,64},{1... | collective-permute-start | bytes 983048 | tf_op jit(solution)/shard_map/ppermute | solution.py:58
  150.3 10.7 %collective-permute-start.47 = (bf16[128,1280]{1,0:T(8,128)(2,1)S(1)}, bf16[128,1280]{1,0:T(8,128)(2,1)S(1)}, u32[]{:S(2)}, u32[]{:S(2)}) collective-permute-start(bf16[128,1280]{1,0:T(8,128)(2,1)S(1)} %add_convert_fusion.4), channel_id=1, source_target_pairs={{0,48},{16,0},{32,16},{48,32},{64,112},{80,64},{96,80},{112,96},{1... | collective-permute-start | bytes 983048 | tf_op jit(solution)/shard_map/ppermute | solution.py:58
  160.5 16.3 %collective-permute-start.38 = (bf16[128,1280]{1,0:T(8,128)(2,1)S(1)}, bf16[128,1280]{1,0:T(8,128)(2,1)S(1)}, u32[]{:S(2)}, u32[]{:S(2)}) collective-permute-start(bf16[128,1280]{1,0:T(8,128)(2,1)S(1)} %slice.97), channel_id=1, source_target_pairs={{0,4},{1,5},{2,6},{3,7},{4,8},{5,9},{6,10},{7,11},{8,12},{9,13},{1... | collective-permute-start | bytes 983048 | tf_op jit(solution)/shard_map/ppermute | solution.py:54
  176.4 11.2 %collective-permute-start.40 = (bf16[128,1280]{1,0:T(8,128)(2,1)S(1)}, bf16[128,1280]{1,0:T(8,128)(2,1)S(1)}, u32[]{:S(2)}, u32[]{:S(2)}) collective-permute-start(bf16[128,1280]{1,0:T(8,128)(2,1)S(1)} %add_convert_fusion.6), channel_id=1, source_target_pairs={{0,12},{1,13},{2,14},{3,15},{4,0},{5,1},{6,2},{7,3},{8,4},{9,5},{1... | collective-permute-start | bytes 983048 | tf_op jit(solution)/shard_map/ppermute | solution.py:54
  176.7 15.5 %collective-permute-start.48 = (bf16[128,1280]{1,0:T(8,128)(2,1)S(1)}, bf16[128,1280]{1,0:T(8,128)(2,1)S(1)}, u32[]{:S(2)}, u32[]{:S(2)}) collective-permute-start(bf16[128,1280]{1,0:T(8,128)(2,1)S(1)} %add_convert_fusion.3), channel_id=1, source_target_pairs={{0,64},{16,80},{32,96},{48,112},{64,0},{80,16},{96,32},{112,48},{1... | collective-permute-start | bytes 983048 | tf_op jit(solution)/shard_map/ppermute | solution.py:58
  (57 other events, 460.6 us)
